TPU v7x, 512 devices: a whole 4x8x8 slice. The times are simulated.
512 devices in a mesh: wide: 128 (over z, y, core), narrow: 4 (over x).
Axes of the slice: x: 4, y: 8, z: 8, core: 2. Of those that a mesh axis runs over, the one named last changes fastest.
Arguments:
- comps: bfloat16 [1024, 512, 128], P('wide', 'narrow'), may hold values from -6 to 6
- entry: int32 [1024, 512], P('wide', 'narrow'), may hold values from 0 to 15
- dest: int32 [128, 4, 1024, 1], P('wide', 'narrow'), may hold values from 0 to 127; in each aligned block of 1024 rows (0 to 1023, 1024 to 2047, ..., all dimensions but the last counted through in order) at most 12 rows name the same one
- slot_of_entry: int32 [128, 4, 16], P('wide', 'narrow'), may hold values from 0 to 15, each once within a row
- table_f0: bfloat16 [128, 4, 16, 128], P('wide', 'narrow'), may hold values from -6 to 6
- table_x0: bfloat16 [128, 4, 16, 128], P('wide', 'narrow'), may hold values from -6 to 6
- table_a: bfloat16 [128, 4, 16, 128, 128], P('wide', 'narrow'), may hold values from -0.5 to 0.5
- courant_x: float32 [1024, 512], P('wide', 'narrow'), may hold values from -0.4 to 0.4
- courant_y: float32 [1024, 512], P('wide', 'narrow'), may hold values from -0.4 to 0.4
- diffusion: float32 [128], replicated, may hold values from 0.02 to 0.1
Outputs:
- transported: float32 [1024, 512, 128], P('wide', 'narrow')
Inputs may be any that keep to these rules, and one draw needn't show every extreme that they name: `dest`: at most 12 cells of one device name the same owner, and exactly 12 do so on some device. `slot_of_entry`: each row is a permutation.
All inputs are finite; a program needn't handle non-finite values.
Results may differ from a plain program's by a relative error of at most 0.0039.
Values may be sent and summed in bfloat16 or wider, within the bound.
A program may use at most 64 MiB of HBM per device.

v0:
```python
import jax
import jax.numpy as jnp
from jax import lax
from jax.sharding import PartitionSpec as P


def with_halo(block, sides, width):
    for axis, dim in sides:
        count = lax.axis_size(axis)
        forward = [(i, i + 1) for i in range(count - 1)]
        backward = [(target, source) for source, target in forward]
        low = lax.ppermute(
            lax.slice_in_dim(block, block.shape[dim] - width, None, axis=dim), axis, forward
        )
        high = lax.ppermute(lax.slice_in_dim(block, 0, width, axis=dim), axis, backward)
        block = jnp.concatenate([low, block, high], axis=dim)
    return block


def transport(padded, courant_x, courant_y, diffusion):
    center = padded[1:-1, 1:-1]
    east = padded[2:, 1:-1]
    west = padded[:-2, 1:-1]
    north = padded[1:-1, 2:]
    south = padded[1:-1, :-2]
    along_x = courant_x[:, :, None]
    along_y = courant_y[:, :, None]
    spread = diffusion[None, None, :]
    result = (
        center
        - 0.5 * along_x * (east - west)
        + (0.5 * along_x * along_x + spread) * (east - 2.0 * center + west)
    )
    return (
        result
        - 0.5 * along_y * (north - south)
        + (0.5 * along_y * along_y + spread) * (north - 2.0 * center + south)
    )


def map_rows(arrived, picks, slot_table, sens_table, base_x_table, base_f_table):
    species = arrived.shape[1]
    table_count = sens_table.shape[0]
    table_ids = jnp.arange(table_count, dtype=jnp.int32)
    is_live = picks >= 0
    looked = jnp.sum(
        jnp.where(picks[:, None] == table_ids[None, :], slot_table[None, :], 0), axis=1
    )
    slots = jnp.where(is_live, looked, -1)

    def one_entry(filled, item):
        entry_id, sens, base_x, base_f = item
        offset = (arrived.astype(jnp.float32) - base_x.astype(jnp.float32)[None, :]).astype(
            jnp.bfloat16
        )
        mapped = base_f.astype(jnp.float32)[None, :] + jnp.dot(
            offset, sens, preferred_element_type=jnp.float32
        )
        return (jnp.where((slots == entry_id)[:, None], mapped, filled), None)

    start = jnp.zeros((arrived.shape[0], species), jnp.float32)
    values, unused = lax.scan(one_entry, start, (table_ids, sens_table, base_x_table, base_f_table))
    return jnp.where(is_live[:, None], values, 0.0).astype(jnp.bfloat16)


def pack_rows(states, entries, targets, ranks, peer_count, room):
    species = states.shape[1]
    kept = jnp.where((ranks >= 0) & (ranks < room), ranks, room)
    send_states = (
        jnp.zeros((peer_count, room, species), jnp.bfloat16)
        .at[targets, kept]
        .set(states, mode="drop")
    )
    send_entries = (
        jnp.full((peer_count, room), -1, jnp.int32).at[targets, kept].set(entries, mode="drop")
    )
    return (send_states, send_entries)


def body(
    comps, entry, dest, slot_of_entry, table_f0, table_x0, table_a, courant_x, courant_y, diffusion
):
    cx_cells, cy_cells, species = comps.shape
    cell_count = cx_cells * cy_cells
    peer_count = lax.axis_size("wide")
    capacity = max(2, 3 * cell_count // (2 * peer_count))
    states = comps.reshape(cell_count, species)
    entries = entry.reshape(cell_count)
    targets = dest.reshape(cell_count)
    onehot = (targets[:, None] == jnp.arange(peer_count, dtype=jnp.int32)[None, :]).astype(
        jnp.int32
    )
    running = jnp.cumsum(onehot, axis=0) - onehot
    slot_rank = jnp.sum(running * onehot, axis=1)
    slot_table = slot_of_entry[0, 0]
    sens_table = table_a[0, 0]
    base_x_table = table_x0[0, 0]
    base_f_table = table_f0[0, 0]
    sent = pack_rows(states, entries, targets, slot_rank, peer_count, capacity)
    piece_states = lax.all_to_all(sent[0], "wide", split_axis=0, concat_axis=0, tiled=True)
    piece_entries = lax.all_to_all(sent[1], "wide", split_axis=0, concat_axis=0, tiled=True)
    item_count = piece_states.shape[1]
    arrived = piece_states.reshape(peer_count * item_count, species)
    picks = piece_entries.reshape(peer_count * item_count)
    values = map_rows(arrived, picks, slot_table, sens_table, base_x_table, base_f_table)
    returned = lax.all_to_all(
        values.reshape(peer_count, item_count, species),
        "wide",
        split_axis=0,
        concat_axis=0,
        tiled=True,
    )
    gathered = returned[targets, slot_rank]
    mine = gathered.reshape(cx_cells, cy_cells, species)
    padded = with_halo(mine, (("wide", 0), ("narrow", 1)), 1)
    return transport(padded.astype(jnp.float32), courant_x, courant_y, diffusion)


def solution(mesh):
    in_specs = (
        P("wide", "narrow", None),
        P("wide", "narrow"),
        P("wide", "narrow", None, None),
        P("wide", "narrow", None),
        P("wide", "narrow", None, None),
        P("wide", "narrow", None, None),
        P("wide", "narrow", None, None, None),
        P("wide", "narrow"),
        P("wide", "narrow"),
        P(),
    )
    out_specs = P("wide", "narrow", None)
    return jax.shard_map(body, mesh=mesh, in_specs=in_specs, out_specs=out_specs, check_vma=False)
```

profile of v0, /device:TPU:1, one launch (start us, length us, event | category | flops | bytes accessed | tf_op | source)
XLA Modules:
  0.0 168.8 jit_solution(3492822678782861246)
XLA Ops:
  0.0 0.8 copy.26
  3.6 4.5 %scatter_custom_fusion = s32[1536]{0:T(1024)S(1)} fusion(s32[1024]{0:T(1024)S(1)} %broadcast_select_fusion.1, s32[1024]{0:T(1024)} %bitcast.70, s32[]{:T(128)} %constant.6.clone.1), kind=kCustom, calls=%fused_computation.50 | custom fusion | bytes 6656
  8.1 0.7 copy.28
  8.8 18.4 %all-to-all-start = ((s32[128,1,12]{2,1,0:T(1,128)}), s32[128,1,12]{2,1,0:T(1,128)S(1)}, u32[]{:S(2)}, u32[]{:S(2)}) async-start(s32[128,1,12]{2,1,0:T(1,128)} %copy.28), calls=%async_computation | async-start | bytes 131072 | tf_op jit(solution)/shard_map/all_to_all | solution.py:101
  27.2 3.6 %scatter_custom_fusion.1 = bf16[1536,128]{1,0:T(8,128)(2,1)S(1)} fusion(s32[1024]{0:T(1024)S(1)} %broadcast_select_fusion.1, bf16[1024,128]{1,0:T(8,128)(2,1)} %bitcast.69, bf16[]{:T(256)} %constant.10.clone.1), kind=kCustom, calls=%fused_computation.29 | custom fusion | bytes 393728
  30.9 1.1 copy.29
  31.9 6.7 %all-to-all-done = s32[128,1,12]{2,1,0:T(1,128)S(1)} async-done(((s32[128,1,12]{2,1,0:T(1,128)}), s32[128,1,12]{2,1,0:T(1,128)S(1)}, u32[]{:S(2)}, u32[]{:S(2)}) %all-to-all-start) | async-done | bytes 6176 | tf_op jit(solution)/shard_map/all_to_all | solution.py:101
  38.7 7.0 %all-to-all-start.1 = ((bf16[128,12,128]{2,1,0:T(8,128)(2,1)}), bf16[128,12,128]{2,1,0:T(8,128)(2,1)S(1)}, u32[]{:S(2)}, u32[]{:S(2)}) async-start(bf16[128,12,128]{2,1,0:T(8,128)(2,1)} %copy.29), calls=%async_computation.1 | async-start | bytes 1048576 | tf_op jit(solution)/shard_map/all_to_all | solution.py:100
  46.2 0.7 reduce.9
  47.8 18.5 %all-to-all-done.1 = bf16[128,12,128]{2,1,0:T(8,128)(2,1)S(1)} async-done(((bf16[128,12,128]{2,1,0:T(8,128)(2,1)}), bf16[128,12,128]{2,1,0:T(8,128)(2,1)S(1)}, u32[]{:S(2)}, u32[]{:S(2)}) %all-to-all-start.1) | async-done | bytes 393248 | tf_op jit(solution)/shard_map/all_to_all | solution.py:100
  66.4 52.5 %while.11 = (s32[]{:T(128)}, bf16[1536,128]{1,0:T(8,128)(2,1)S(1)}, s32[16]{0:T(128)S(1)}, s32[1536]{0:T(1024)S(1)}, bf16[16,128]{1,0:T(8,128)(2,1)}, /*index=5*...) while((s32[]{:T(128)}, bf16[1536,128]{1,0:T(8,128)(2,1)S(1)}, ...), condition=%wide.region_7.8_spmd.clone, body=%wide.region_6.7_spmd.clone.sunk | while | flops 51513088 | bytes 1224835 | solution.py:62
  66.4 0.7 fusion.27
  68.3 1.3 fusion.28
  69.7 0.7 fusion.27
  71.6 1.3 fusion.28
  72.9 0.7 fusion.27
  74.9 1.3 fusion.28
  76.2 0.7 fusion.27
  78.2 1.3 fusion.28
  79.5 0.7 fusion.27
  81.5 1.3 fusion.28
  82.8 0.7 fusion.27
  84.8 1.3 fusion.28
  86.1 0.7 fusion.27
  88.0 1.3 fusion.28
  89.4 0.7 fusion.27
  91.3 1.3 fusion.28
  92.7 0.7 fusion.27
  94.6 1.3 fusion.28
  95.9 0.7 fusion.27
  97.9 1.3 fusion.28
  99.2 0.7 fusion.27
  101.2 1.3 fusion.28
  102.5 0.7 fusion.27
  104.5 1.3 fusion.28
  107.7 1.3 fusion.28
  111.0 1.3 fusion.28
  114.3 1.3 fusion.28
  117.6 1.3 fusion.28
  119.3 25.8 %all_to_all.19 = bf16[128,12,128]{2,1,0:T(8,128)(2,1)S(1)} all-to-all(bf16[128,12,128]{2,1,0:T(8,128)(2,1)S(1)} %reshape.136), channel_id=1, replica_groups=mesh['wide'=128,'narrow'=4] {'wide'}, dimensions={0} | all-to-all | bytes 786432 | tf_op jit(solution)/shard_map/all_to_all | solution.py:106
  145.2 5.6 %gather_fusion = bf16[1024,128]{1,0:T(8,128)(2,1)S(1)} fusion(bf16[128,12,128]{2,0,1:T(8,128)(2,1)S(1)} %copy.30, s32[1024]{0:T(1024)S(1)} %bitcast.57), kind=kCustom, calls=%fused_computation | custom fusion | bytes 532480 | tf_op jit(solution)/shard_map/gather | solution.py:113
  150.8 3.2 %collective-permute-start = (bf16[1,128,128]{2,1,0:T(8,128)(2,1)S(1)}, bf16[1,128,128]{2,1,0:T(8,128)(2,1)S(1)}, u32[]{:S(2)}, u32[]{:S(2)}) collective-permute-start(bf16[1,128,128]{2,1,0:T(8,128)(2,1)S(1)} %get-tuple-element.97), channel_id=1, source_target_pairs={{0,4},{4,8},{8,12},{12,16},{16,20},{20,24},{24,28},{28,32},{32,36}... | collective-permute-start | bytes 98312 | tf_op jit(solution)/shard_map/ppermute | solution.py:12
  153.9 1.9 %collective-permute-start.1 = (bf16[1,128,128]{2,1,0:T(8,128)(2,1)S(1)}, bf16[1,128,128]{2,1,0:T(8,128)(2,1)S(1)}, u32[]{:S(2)}, u32[]{:S(2)}) collective-permute-start(bf16[1,128,128]{2,1,0:T(8,128)(2,1)S(1)} %get-tuple-element.98), channel_id=1, source_target_pairs={{4,0},{8,4},{12,8},{16,12},{20,16},{24,20},{28,24},{32,28},{36,32}... | collective-permute-start | bytes 98312 | tf_op jit(solution)/shard_map/ppermute | solution.py:15
  155.9 3.3 %collective-permute-done.1 = bf16[1,128,128]{2,1,0:T(8,128)(2,1)S(1)} collective-permute-done((bf16[1,128,128]{2,1,0:T(8,128)(2,1)S(1)}, bf16[1,128,128]{2,1,0:T(8,128)(2,1)S(1)}, u32[]{:S(2)}, u32[]{:S(2)}) %collective-permute-start.1) | collective-permute-done | bytes 32800 | tf_op jit(solution)/shard_map/ppermute | solution.py:15
  159.2 3.1 %collective-permute-start.2 = (bf16[10,1,128]{2,1,0:T(2,128)(2,1)S(1)}, bf16[10,1,128]{2,1,0:T(2,128)(2,1)S(1)}, u32[]{:S(2)}, u32[]{:S(2)}) collective-permute-start(bf16[10,1,128]{2,1,0:T(2,128)(2,1)S(1)} %get-tuple-element.95), channel_id=1, source_target_pairs={{0,1},{1,2},{2,3},{4,5},{5,6},{6,7},{8,9},{9,10},{10,11},{12,13},{... | collective-permute-start | bytes 7688 | tf_op jit(solution)/shard_map/ppermute | solution.py:12
  162.3 1.3 collective-permute-start.3
  163.7 3.0 %collective-permute-done.3 = bf16[10,1,128]{2,1,0:T(2,128)(2,1)S(1)} collective-permute-done((bf16[10,1,128]{2,1,0:T(2,128)(2,1)S(1)}, bf16[10,1,128]{2,1,0:T(2,128)(2,1)S(1)}, u32[]{:S(2)}, u32[]{:S(2)}) %collective-permute-start.3) | collective-permute-done | bytes 2592 | tf_op jit(solution)/shard_map/ppermute | solution.py:15
  167.4 1.4 multiply_add_fusion
  (77 shorter events, 28.0 us)
Async XLA Ops:
  1.1 0.7 copy-start
  2.2 0.7 copy-start.5
  2.8 0.7 copy-start.4
  8.8 29.9 %all-to-all-start = ((s32[128,1,12]{2,1,0:T(1,128)}), s32[128,1,12]{2,1,0:T(1,128)S(1)}, u32[]{:S(2)}, u32[]{:S(2)}) async-start(s32[128,1,12]{2,1,0:T(1,128)} %copy.28), calls=%async_computation | async-start | bytes 131072 | tf_op jit(solution)/shard_map/all_to_all | solution.py:101
  38.7 27.6 %all-to-all-start.1 = ((bf16[128,12,128]{2,1,0:T(8,128)(2,1)}), bf16[128,12,128]{2,1,0:T(8,128)(2,1)S(1)}, u32[]{:S(2)}, u32[]{:S(2)}) async-start(bf16[128,12,128]{2,1,0:T(8,128)(2,1)} %copy.29), calls=%async_computation.1 | async-start | bytes 1048576 | tf_op jit(solution)/shard_map/all_to_all | solution.py:100
  47.0 0.7 copy-start.3
  150.8 5.1 %collective-permute-start = (bf16[1,128,128]{2,1,0:T(8,128)(2,1)S(1)}, bf16[1,128,128]{2,1,0:T(8,128)(2,1)S(1)}, u32[]{:S(2)}, u32[]{:S(2)}) collective-permute-start(bf16[1,128,128]{2,1,0:T(8,128)(2,1)S(1)} %get-tuple-element.97), channel_id=1, source_target_pairs={{0,4},{4,8},{8,12},{12,16},{16,20},{20,24},{24,28},{28,32},{32,36}... | collective-permute-start | bytes 98312 | tf_op jit(solution)/shard_map/ppermute | solution.py:12
  153.9 5.2 %collective-permute-start.1 = (bf16[1,128,128]{2,1,0:T(8,128)(2,1)S(1)}, bf16[1,128,128]{2,1,0:T(8,128)(2,1)S(1)}, u32[]{:S(2)}, u32[]{:S(2)}) collective-permute-start(bf16[1,128,128]{2,1,0:T(8,128)(2,1)S(1)} %get-tuple-element.98), channel_id=1, source_target_pairs={{4,0},{8,4},{12,8},{16,12},{20,16},{24,20},{28,24},{32,28},{36,32}... | collective-permute-start | bytes 98312 | tf_op jit(solution)/shard_map/ppermute | solution.py:15
  159.2 4.4 %copy-start.1 = (f32[8,128]{1,0:T(8,128)S(1)}, f32[8,128]{1,0:T(8,128)}, u32[]{:S(2)}) copy-start(f32[8,128]{1,0:T(8,128)} %param.20) | copy-start | bytes 12292
  159.2 4.5 %copy-start.2 = (f32[8,128]{1,0:T(8,128)S(1)}, f32[8,128]{1,0:T(8,128)}, u32[]{:S(2)}) copy-start(f32[8,128]{1,0:T(8,128)} %param.19) | copy-start | bytes 12292
  159.2 4.5 %collective-permute-start.2 = (bf16[10,1,128]{2,1,0:T(2,128)(2,1)S(1)}, bf16[10,1,128]{2,1,0:T(2,128)(2,1)S(1)}, u32[]{:S(2)}, u32[]{:S(2)}) collective-permute-start(bf16[10,1,128]{2,1,0:T(2,128)(2,1)S(1)} %get-tuple-element.95), channel_id=1, source_target_pairs={{0,1},{1,2},{2,3},{4,5},{5,6},{6,7},{8,9},{9,10},{10,11},{12,13},{... | collective-permute-start | bytes 7688 | tf_op jit(solution)/shard_map/ppermute | solution.py:12
  162.3 4.4 %collective-permute-start.3 = (bf16[10,1,128]{2,1,0:T(2,128)(2,1)S(1)}, bf16[10,1,128]{2,1,0:T(2,128)(2,1)S(1)}, u32[]{:S(2)}, u32[]{:S(2)}) collective-permute-start(bf16[10,1,128]{2,1,0:T(2,128)(2,1)S(1)} %get-tuple-element.96), channel_id=1, source_target_pairs={{1,0},{2,1},{3,2},{5,4},{6,5},{7,6},{9,8},{10,9},{11,10},{13,12},{... | collective-permute-start | bytes 7688 | tf_op jit(solution)/shard_map/ppermute | solution.py:15
  166.8 0.7 copy-start.6
where the time goes:
time: 171 us; the launch traced here: 169 us
  starting transfers between devices  34.9 us (20%)
  waiting for transfers between devices  31.5 us (18%)
  local copies, waits for them, and re-layouts  29.7 us (17%)
  blocking collectives  25.8 us (15%)
  other arithmetic  25.1 us (15%)
  matrix products  21.1 us (12%)
    all_to_all x1, blocking collectives, body(): lax.all_to_all(values.reshape(peer_count, item_count, species), 'wide', s...  25.8 us
    dot_general x16, matrix products, one_entry(): jnp.dot(offset, sens, preferred_element_type=jnp.float32)  21.1 us
    all_to_all x1, waiting for transfers between devices, body(): lax.all_to_all(sent[0], 'wide', split_axis=0, concat_axis=0, tiled=True)  18.5 us
    all_to_all x1, starting transfers between devices, body(): lax.all_to_all(sent[1], 'wide', split_axis=0, concat_axis=0, tiled=True)  18.4 us
    add x16, other arithmetic, one_entry(): base_f.astype(jnp.float32)[None, :]  11.3 us
    unnamed x16, local copies, waits for them, and re-layouts  11.2 us
    eq x16, other arithmetic, one_entry(): return (jnp.where((slots == entry_id)[:, None], mapped, filled), None)  10.4 us
    dynamic_slice x16, local copies, waits for them, and re-layouts, map_rows(): lax.scan(one_entry, start, (table_ids, sens_table, base_x_table, base_f_t...  9.31 us
  transfers between devices with their start and end apart: 6, of which 4 were waited for; matrix products, arithmetic and copies ran while one was open for 4% of the time, Pallas kernels for 0%

commit v1 on v0

v1 whole, which is shorter than its diff:
```python
import jax
import jax.numpy as jnp
from jax import lax
from jax.experimental import pallas as pl
from jax.experimental.pallas import tpu as pltpu
from jax.sharding import PartitionSpec as P

MESH = pl.DeviceIdType.MESH
F32 = jnp.float32
BF16 = jnp.bfloat16

SIDE = 8
SELF = 7
CAP = 12
SLAB = 32
SENT = 26
BACK = 24
ENTRY_ROW = 24
SLABS = 64
GROUP = 8 * SLAB
ENTRIES = 16


def far_first(i):
    odd = i % 2
    return (4 + odd * ((i + 1) // 2) + (1 - odd) * (8 - i // 2)) % SIDE


def rank_of_distance(d):
    t = lax.rem(d + 7, SIDE) - 3
    return jnp.where(t > 0, 2 * t - 1, -2 * t)


def iota(shape, dim):
    return lax.broadcasted_iota(jnp.int32, shape, dim)


def dot(a, b):
    return jnp.dot(a, b, preferred_element_type=F32)


def onehot(match):
    return jnp.where(match, 1.0, 0.0).astype(BF16)


def kernel(
    comps, entry, dest, slots, f0, x0, sens, cour_x, cour_y, diffusion, out,
    send, recv, res, ret, tab_a, tab_xf, col_p, acc, halo_src, halo_dst, edge_src, edge_dst,
    fwd_send, fwd_recv, ret_send, ret_recv, tab_send, tab_recv, halo_send, halo_recv,
):
    me = lax.axis_index("wide")
    mine_n = lax.axis_index("narrow")
    z, y, c = me // 16, (me // 2) % SIDE, me % 2

    def at(dz, dy):
        return {"wide": ((z + dz) % SIDE) * 16 + ((y + dy) % SIDE) * 2 + c}

    def ahead(a, b):
        return at(far_first((a + b) % SIDE), far_first(b))

    def behind(a, b):
        return at(SIDE - far_first((a + b) % SIDE), SIDE - far_first(b))

    def each_group(step):
        step(0, SIDE - 1)

        def body(a, carry):
            step(a, SIDE)
            return carry

        lax.fori_loop(1, SIDE, body, 0)

    partner = {"wide": me + 1 - 2 * c}
    above, below = {"wide": (me + 1) % 128}, {"wide": (me + 127) % 128}
    north, south = {"narrow": (mine_n + 1) % 4}, {"narrow": (mine_n + 3) % 4}

    recv[...] = jnp.zeros_like(recv)
    ret[...] = jnp.zeros_like(ret)
    tab_xf[pl.ds(32, 96), :] = jnp.zeros((96, 256), BF16)

    barrier = pltpu.get_barrier_semaphore()

    def greet(device):
        pl.semaphore_signal(barrier, inc=1, device_id=device, device_id_type=MESH)

    def greet_group(a, peers):
        for b in range(peers):
            greet(ahead(a, b))

    each_group(greet_group)
    for device in (partner, above, below, north, south):
        greet(device)

    pick = jnp.zeros((ENTRIES, 128), F32)
    for e in range(ENTRIES):
        s = slots[e]
        tab_a[c, pl.ds(e * 128, 128), :] = sens[s]
        pick = jnp.where((iota(pick.shape, 0) == e) & (iota(pick.shape, 1) == s), 1.0, pick)
    xf = jnp.concatenate([x0[...], f0[...]], axis=1)
    xf = jnp.concatenate([xf, jnp.zeros((112, 256), BF16)], axis=0)
    own_rows = pl.ds(pl.multiple_of(c * ENTRIES, ENTRIES), ENTRIES)
    tab_xf[own_rows, :] = dot(pick.astype(BF16), xf).astype(BF16)

    owner = dest[...]
    matches = [iota((128, 128), 0) == owner[i : i + 1, :] for i in range(8)]
    owned = jnp.concatenate([onehot(m) for m in matches], axis=0)
    before = onehot(iota((128, 128), 0) < iota((128, 128), 1))
    counts = dot(owned, jnp.concatenate([before, jnp.ones((128, 128), BF16)], axis=1))
    carry = jnp.zeros((128, 128), F32)
    ranks = []
    for i in range(8):
        part = counts[i * 128 : (i + 1) * 128]
        seen = jnp.where(matches[i], part[:, :128] + carry, 0.0)
        ranks.append(jnp.sum(seen, axis=0, keepdims=True))
        carry = carry + part[:, 128:]
    rank = jnp.concatenate(ranks, axis=0).astype(jnp.int32)

    to_core = owner % 2
    i_y = rank_of_distance((owner // 2 + SIDE - y) % SIDE)
    i_z = rank_of_distance((owner // 16 + SIDE - z) % SIDE)
    slab = ((i_z + SIDE - i_y) % SIDE) * SIDE + i_y
    row = to_core * CAP + rank
    place = slab * SLAB + row
    named = entry[...] + to_core * ENTRIES + 1

    place_t = jnp.transpose(place.astype(F32))
    row_t = jnp.transpose(row.astype(F32))
    named_t = jnp.transpose(named.astype(F32))
    lane = iota((128, 128), 1)
    lane_f = lane.astype(F32)
    names = []
    for i in range(8):
        col_p[pl.ds(i * 128, 128), :] = jnp.broadcast_to(place_t[:, i : i + 1], (128, 128))
        at_row = jnp.broadcast_to(row_t[:, i : i + 1], (128, 128)) == lane_f
        names.append(jnp.where(at_row, jnp.broadcast_to(named_t[:, i : i + 1], (128, 128)), 0.0))
    names = jnp.concatenate(names, axis=0).astype(BF16)
    in_slab = jnp.concatenate([onehot(iota((128, 128), 0) == slab[i : i + 1, :]) for i in range(8)], axis=1)
    entry_rows = dot(in_slab, names).astype(BF16)
    entry_place = jnp.where(lane[:1] < SLABS, lane[:1] * SLAB + ENTRY_ROW, -1)
    cells = jnp.concatenate([comps[...].reshape(1024, 128), entry_rows], axis=0)
    places = [place[i : i + 1, :] for i in range(8)] + [entry_place]

    def pack(a, carry):
        slot = iota((GROUP, 128), 0) + a * GROUP
        chosen = jnp.concatenate([onehot(slot == p) for p in places], axis=1)
        send[pl.ds(a * 8, 8)] = dot(chosen, cells).astype(BF16).reshape(8, SLAB, 128)
        return carry

    lax.fori_loop(0, SIDE, pack, 0)
    recv[SELF] = send[SELF]

    pl.semaphore_wait(barrier, SLABS - 1 + 5)

    def send_group(a, peers):
        for b in range(peers):
            pltpu.make_async_remote_copy(
                src_ref=send.at[a * 8 + b, pl.ds(0, SENT)],
                dst_ref=recv.at[a * 8 + b, pl.ds(0, SENT)],
                send_sem=fwd_send,
                recv_sem=fwd_recv.at[a],
                device_id=ahead(a, b),
                device_id_type=MESH,
            ).start()

    each_group(send_group)

    swaps = []
    for n, ref in enumerate((tab_a.at[c], tab_xf.at[own_rows])):
        swap = pltpu.make_async_remote_copy(
            src_ref=ref,
            dst_ref=ref,
            send_sem=tab_send.at[n],
            recv_sem=tab_recv.at[n],
            device_id=partner,
            device_id_type=MESH,
        )
        swap.start()
        swaps.append(swap)
    for swap in swaps:
        swap.wait()

    def wait_for(ref, sem):
        pltpu.make_async_copy(ref, ref, sem).wait()

    wide_lane = iota((GROUP, 128), 1)
    in_own_row = wide_lane == iota((GROUP, 128), 0) % SLAB
    spread = onehot(iota((GROUP, GROUP), 1) == (iota((GROUP, GROUP), 0) // SLAB) * SLAB + ENTRY_ROW)
    all_ones = jnp.ones((128, 128), BF16)

    def map_group(a, peers):
        wait_for(recv.at[pl.ds(a * 8, peers), pl.ds(0, SENT)], fwd_recv.at[a])
        states = recv[pl.ds(a * 8, 8)].reshape(GROUP, 128)
        named = jnp.where(in_own_row, dot(spread, states), 0.0).astype(BF16)
        named = dot(named, all_ones)
        base = dot(onehot(named == (wide_lane + 1).astype(F32)), tab_xf[...])
        offset = (states.astype(F32) - base[:, :128]).astype(BF16)
        chosen = [
            jnp.where(named == float(e + 1), offset.astype(F32), 0.0).astype(BF16) for e in range(2 * ENTRIES)
        ]
        moved = dot(jnp.concatenate(chosen, axis=1), tab_a[...].reshape(2 * ENTRIES * 128, 128))
        res[pl.ds(a * 8, 8)] = (base[:, 128:] + moved).astype(BF16).reshape(8, SLAB, 128)
        for b in range(peers):
            pltpu.make_async_remote_copy(
                src_ref=res.at[a * 8 + b, pl.ds(0, BACK)],
                dst_ref=ret.at[a * 8 + b, pl.ds(0, BACK)],
                send_sem=ret_send,
                recv_sem=ret_recv.at[a],
                device_id=behind(a, b),
                device_id_type=MESH,
            ).start()

    each_group(map_group)
    ret[SELF] = res[SELF]

    def placed(a, first, count):
        slot = (iota((count, 128), 1) + a * GROUP).astype(F32)
        at_col = col_p[pl.ds(first, count), :]
        chosen = jnp.concatenate([onehot(at_col == slot), onehot(at_col == slot + 128.0)], axis=1)
        return dot(chosen, ret[pl.ds(a * 8, 8)].reshape(GROUP, 128))

    acc[...] = jnp.zeros_like(acc)

    def place_group(a, peers):
        wait_for(ret.at[pl.ds(a * 8, peers), pl.ds(0, BACK)], ret_recv.at[a])
        acc[...] += placed(a, 0, 1024)

    each_group(place_group)

    halo_src[0] = acc[pl.ds(0, 128), :].astype(BF16)
    halo_src[1] = acc[pl.ds(896, 128), :].astype(BF16)
    field = [acc[pl.ds(i * 128, 128), :] for i in range(8)]
    edge_src[0] = jnp.concatenate([p[:1] for p in field], axis=0)
    edge_src[1] = jnp.concatenate([p[127:] for p in field], axis=0)
    halos = []
    for n, (src, dst, device) in enumerate(
        (
            (halo_src.at[0], halo_dst.at[1], below),
            (halo_src.at[1], halo_dst.at[0], above),
            (edge_src.at[0], edge_dst.at[1], south),
            (edge_src.at[1], edge_dst.at[0], north),
        )
    ):
        halo = pltpu.make_async_remote_copy(
            src_ref=src,
            dst_ref=dst,
            send_sem=halo_send.at[n],
            recv_sem=halo_recv.at[n],
            device_id=device,
            device_id_type=MESH,
        )
        halo.start()
        halos.append(halo)

    for halo in halos:
        halo.wait()

    spread_k = diffusion[...]
    cx_t = jnp.transpose(cour_x[...])
    cy_t = jnp.transpose(cour_y[...])
    low = jnp.where(me > 0, halo_dst[0].astype(F32), 0.0)
    high = jnp.where(me < 127, halo_dst[1].astype(F32), 0.0)
    edge_s = jnp.where(mine_n > 0, edge_dst[0], 0.0)
    edge_n = jnp.where(mine_n < 3, edge_dst[1], 0.0)
    for i in range(8):
        p = field[i]
        west = field[i - 1] if i > 0 else low
        east = field[i + 1] if i < 7 else high
        pn = jnp.concatenate([p[1:], edge_n[i : i + 1]], axis=0)
        ps = jnp.concatenate([edge_s[i : i + 1], p[:127]], axis=0)
        cx = jnp.broadcast_to(cx_t[:, i : i + 1], (128, 128))
        cy = jnp.broadcast_to(cy_t[:, i : i + 1], (128, 128))
        r = p - 0.5 * cx * (east - west) + (0.5 * cx * cx + spread_k) * (east - 2.0 * p + west)
        out[i] = r - 0.5 * cy * (pn - ps) + (0.5 * cy * cy + spread_k) * (pn - 2.0 * p + ps)

    for first, count in ((0, SELF), (SIDE, SLABS - SIDE)):
        wait_for(send.at[pl.ds(first, count), pl.ds(0, SENT)], fwd_send)
        wait_for(res.at[pl.ds(first, count), pl.ds(0, BACK)], ret_send)


def body(comps, entry, dest, slot_of_entry, table_f0, table_x0, table_a, courant_x, courant_y, diffusion):
    vmem = pl.BlockSpec(memory_space=pltpu.VMEM)
    smem = pl.BlockSpec(memory_space=pltpu.SMEM)
    dma = pltpu.SemaphoreType.DMA
    return pl.pallas_call(
        kernel,
        out_shape=jax.ShapeDtypeStruct(comps.shape, F32),
        in_specs=[vmem, vmem, vmem, smem] + [vmem] * 6,
        out_specs=vmem,
        scratch_shapes=[
            pltpu.VMEM((SLABS, SLAB, 128), BF16),
            pltpu.VMEM((SLABS, SLAB, 128), BF16),
            pltpu.VMEM((SLABS, SLAB, 128), BF16),
            pltpu.VMEM((SLABS, SLAB, 128), BF16),
            pltpu.VMEM((2, ENTRIES * 128, 128), BF16),
            pltpu.VMEM((128, 256), BF16),
            pltpu.VMEM((1024, 128), F32),
            pltpu.VMEM((1024, 128), F32),
            pltpu.VMEM((2, 128, 128), BF16),
            pltpu.VMEM((2, 128, 128), BF16),
            pltpu.VMEM((2, 8, 128), F32),
            pltpu.VMEM((2, 8, 128), F32),
            dma(()),
            dma((SIDE,)),
            dma(()),
            dma((SIDE,)),
            dma((2,)),
            dma((2,)),
            dma((4,)),
            dma((4,)),
        ],
        compiler_params=pltpu.CompilerParams(
            collective_id=0, has_side_effects=True, vmem_limit_bytes=48 * 1024 * 1024
        ),
        name="chemistry",
    )(
        comps,
        entry,
        dest.reshape(entry.shape),
        slot_of_entry.reshape(ENTRIES),
        table_f0[0, 0],
        table_x0[0, 0],
        table_a[0, 0],
        courant_x,
        courant_y,
        diffusion.reshape(1, -1),
    )


def solution(mesh):
    in_specs = (
        P("wide", "narrow", None),
        P("wide", "narrow"),
        P("wide", "narrow", None, None),
        P("wide", "narrow", None),
        P("wide", "narrow", None, None),
        P("wide", "narrow", None, None),
        P("wide", "narrow", None, None, None),
        P("wide", "narrow"),
        P("wide", "narrow"),
        P(),
    )
    out_specs = P("wide", "narrow", None)
    return jax.shard_map(body, mesh=mesh, in_specs=in_specs, out_specs=out_specs, check_vma=False)
```

time: 171 us -> 52.8 us (0.31); the launches traced: 169 us -> 52.4 us
  Pallas kernels: 0 us -> 46.1 us
  starting transfers between devices: 34.9 us -> 0 us
  waiting for transfers between devices: 31.5 us -> 0 us
  blocking collectives: 25.8 us -> 0 us
  other arithmetic: 25.1 us -> 0 us
  local copies, waits for them, and re-layouts: 29.7 us -> 6.23 us
  matrix products: 21.1 us -> 0 us
    pallas_call x0 -> x1, Pallas kernels: none -> 46.1 us  [body(): pl.pallas_call(kernel, out_shape=jax.ShapeDtypeStruct(comps.shape, F32),...]
    all_to_all x1 -> x0, blocking collectives: 25.8 us -> none  [body(): lax.all_to_all(values.reshape(peer_count, item_count, species), 'wide', s...]
    all_to_all x2 -> x0, starting transfers between devices: 25.4 us -> none  [the longest x1 18.4 us: body(): lax.all_to_all(sent[1], 'wide', split_axis=0, concat_axis=0, tiled=True)]
    all_to_all x2 -> x0, waiting for transfers between devices: 25.2 us -> none  [the longest x1 18.5 us: body(): lax.all_to_all(sent[0], 'wide', split_axis=0, concat_axis=0, tiled=True)]
    dot_general x16 -> x0, matrix products: 21.1 us -> none  [one_entry(): jnp.dot(offset, sens, preferred_element_type=jnp.float32)]
    add x17 -> x0, other arithmetic: 12.7 us -> none  [the longest x16 11.3 us: one_entry(): base_f.astype(jnp.float32)[None, :]]
    eq x16 -> x0, other arithmetic: 10.4 us -> none  [one_entry(): return (jnp.where((slots == entry_id)[:, None], mapped, filled), None)]
    ppermute x4 -> x0, starting transfers between devices: 9.48 us -> none  [the longest x2 6.27 us: with_halo(): lax.ppermute(lax.slice_in_dim(block, block.shape[dim] - width, None, axis...]
  transfers between devices with their start and end apart: 6 -> 0, of which waited for: 4 -> 0; matrix products, arithmetic and copies ran while one was open for 4% -> 0% of each run, Pallas kernels for 0% -> 0%
where the time goes in v1:
time: 52.8 us; the launch traced here: 52.4 us
  Pallas kernels  46.1 us (87%)
  local copies, waits for them, and re-layouts  6.23 us (12%)
    pallas_call x1, Pallas kernels, body(): pl.pallas_call(kernel, out_shape=jax.ShapeDtypeStruct(comps.shape, F32),...  46.1 us
    unnamed x21, local copies, waits for them, and re-layouts  6.23 us

profile of v1, /device:TPU:1, one launch (start us, length us, event | category | flops | bytes accessed | tf_op | source)
XLA Modules:
  0.0 52.4 jit_solution(3568882163910144176)
XLA Ops:
  0.0 0.0 copy-start.3
  0.0 0.0 copy-start.2
  0.0 0.0 copy-start.8
  0.0 0.0 copy-start.9
  0.0 0.7 %copy-done.3 = s32[1,1,1024,1]{2,3,1,0:T(1,128)S(1)} copy-done((s32[1,1,1024,1]{2,3,1,0:T(1,128)S(1)}, s32[1,1,1024,1]{2,3,1,0:T(1,128)}, u32[]{:S(2)}) %copy-start.3) | copy-done | bytes 4120
  0.7 0.0 copy-done.2
  0.7 0.0 copy-done.8
  0.7 0.0 copy-done.9
  0.7 0.0 copy-start
  0.7 1.0 %copy-done = bf16[1,1,16,128,128]{4,3,2,1,0:T(8,128)(2,1)S(1)} copy-done((bf16[1,1,16,128,128]{4,3,2,1,0:T(8,128)(2,1)S(1)}, bf16[1,1,16,128,128]{4,3,2,1,0:T(8,128)(2,1)}, u32[]{:S(2)}) %copy-start) | copy-done | bytes 524312
  1.8 0.0 copy-start.1
  1.8 0.9 %copy-done.1 = bf16[8,128,128]{2,1,0:T(8,128)(2,1)S(1)} copy-done((bf16[8,128,128]{2,1,0:T(8,128)(2,1)S(1)}, bf16[8,128,128]{2,1,0:T(8,128)(2,1)}, u32[]{:S(2)}) %copy-start.1) | copy-done | bytes 262168
  2.7 0.0 copy-start.4
  2.7 0.7 %copy-done.4 = bf16[1,1,16,128]{3,2,1,0:T(8,128)(2,1)S(1)} copy-done((bf16[1,1,16,128]{3,2,1,0:T(8,128)(2,1)S(1)}, bf16[1,1,16,128]{3,2,1,0:T(8,128)(2,1)}, u32[]{:S(2)}) %copy-start.4) | copy-done | bytes 4120
  3.4 0.0 copy-start.5
  3.4 0.7 %copy-done.5 = bf16[1,1,16,128]{3,2,1,0:T(8,128)(2,1)S(1)} copy-done((bf16[1,1,16,128]{3,2,1,0:T(8,128)(2,1)S(1)}, bf16[1,1,16,128]{3,2,1,0:T(8,128)(2,1)}, u32[]{:S(2)}) %copy-start.5) | copy-done | bytes 4120
  4.1 0.0 copy-start.6
  4.1 0.7 %copy-done.6 = f32[8,128]{1,0:T(8,128)S(1)} copy-done((f32[8,128]{1,0:T(8,128)S(1)}, f32[8,128]{1,0:T(8,128)}, u32[]{:S(2)}) %copy-start.6) | copy-done | bytes 4120
  4.8 0.0 copy-start.7
  4.8 0.7 %copy-done.7 = f32[8,128]{1,0:T(8,128)S(1)} copy-done((f32[8,128]{1,0:T(8,128)S(1)}, f32[8,128]{1,0:T(8,128)}, u32[]{:S(2)}) %copy-start.7) | copy-done | bytes 4120
  5.5 46.1 %chemistry.1 = f32[8,128,128]{2,1,0:T(8,128)S(1)} custom-call(bf16[8,128,128]{2,1,0:T(8,128)(2,1)S(1)} %copy-done.1, s32[8,128]{1,0:T(8,128)S(1)} %copy-done.2, s32[8,128]{1,0:T(8,128)S(1)} %bitcast.7, s32[16]{0:T(128)S(1)} %bitcast.10, bf16[16,128]{1,0:T(8,128)(2,1)S(1)} %bitcast.8, bf16[16,128]{1,0:T(8,128)(2,1)S(1)} %bitcast.9, ...), custom_call_target="tpu_custom_call" | custom-call | tf_op jit(solution)/shard_map/chemistry/pallas_call | solution.py:284
  51.6 0.8 %copy.12 = f32[8,128,128]{2,1,0:T(8,128)} copy(f32[8,128,128]{2,1,0:T(8,128)S(1)} %chemistry.1) | data formatting | bytes 1048576
Async XLA Ops:
  0.0 0.7 %copy-start.3 = (s32[1,1,1024,1]{2,3,1,0:T(1,128)S(1)}, s32[1,1,1024,1]{2,3,1,0:T(1,128)}, u32[]{:S(2)}) copy-start(s32[1,1,1024,1]{2,3,1,0:T(1,128)} %param.12) | copy-start | bytes 12292
  0.0 0.7 %copy-start.2 = (s32[8,128]{1,0:T(8,128)S(1)}, s32[8,128]{1,0:T(8,128)}, u32[]{:S(2)}) copy-start(s32[8,128]{1,0:T(8,128)} %entry.1) | copy-start | bytes 12292
  0.0 0.7 %copy-start.8 = (s32[1,1,16]{2,1,0:T(1,128)S(1)}, s32[1,1,16]{2,1,0:T(1,128)}, u32[]{:S(2)}) copy-start(s32[1,1,16]{2,1,0:T(1,128)} %param.13) | copy-start | bytes 196
  0.0 0.7 %copy-start.9 = (f32[128]{0:T(128)S(1)}, f32[128]{0:T(128)}, u32[]{:S(2)}) copy-start(f32[128]{0:T(128)} %param.19) | copy-start | bytes 1540
  0.7 1.0 %copy-start = (bf16[1,1,16,128,128]{4,3,2,1,0:T(8,128)(2,1)S(1)}, bf16[1,1,16,128,128]{4,3,2,1,0:T(8,128)(2,1)}, u32[]{:S(2)}) copy-start(bf16[1,1,16,128,128]{4,3,2,1,0:T(8,128)(2,1)} %param.16) | copy-start | bytes 1572868
  1.8 0.9 %copy-start.1 = (bf16[8,128,128]{2,1,0:T(8,128)(2,1)S(1)}, bf16[8,128,128]{2,1,0:T(8,128)(2,1)}, u32[]{:S(2)}) copy-start(bf16[8,128,128]{2,1,0:T(8,128)(2,1)} %comps.1) | copy-start | bytes 786436
  2.7 0.7 %copy-start.4 = (bf16[1,1,16,128]{3,2,1,0:T(8,128)(2,1)S(1)}, bf16[1,1,16,128]{3,2,1,0:T(8,128)(2,1)}, u32[]{:S(2)}) copy-start(bf16[1,1,16,128]{3,2,1,0:T(8,128)(2,1)} %param.14) | copy-start | bytes 12292
  3.4 0.7 %copy-start.5 = (bf16[1,1,16,128]{3,2,1,0:T(8,128)(2,1)S(1)}, bf16[1,1,16,128]{3,2,1,0:T(8,128)(2,1)}, u32[]{:S(2)}) copy-start(bf16[1,1,16,128]{3,2,1,0:T(8,128)(2,1)} %param.15) | copy-start | bytes 12292
  4.1 0.7 %copy-start.6 = (f32[8,128]{1,0:T(8,128)S(1)}, f32[8,128]{1,0:T(8,128)}, u32[]{:S(2)}) copy-start(f32[8,128]{1,0:T(8,128)} %cour_x.1) | copy-start | bytes 12292
  4.8 0.7 %copy-start.7 = (f32[8,128]{1,0:T(8,128)S(1)}, f32[8,128]{1,0:T(8,128)}, u32[]{:S(2)}) copy-start(f32[8,128]{1,0:T(8,128)} %cour_y.1) | copy-start | bytes 12292

commit v2 on v1

v2 whole, which is shorter than its diff:
```python
import jax
import jax.numpy as jnp
from jax import lax
from jax.experimental import pallas as pl
from jax.experimental.pallas import tpu as pltpu
from jax.sharding import PartitionSpec as P

MESH = pl.DeviceIdType.MESH
F32 = jnp.float32
BF16 = jnp.bfloat16

SIDE = 8
SELF = 55
SELF_GROUP = SELF // SIDE
CAP = 12
SLAB = 32
SENT = 26
BACK = 24
ENTRY_ROW = 24
SLABS = 64
GROUP = 8 * SLAB
ENTRIES = 16


def far_first(i):
    odd = i % 2
    return (4 + odd * ((i + 1) // 2) + (1 - odd) * (8 - i // 2)) % SIDE


def rank_of_distance(d):
    t = lax.rem(d + 7, SIDE) - 3
    return jnp.where(t > 0, 2 * t - 1, -2 * t)


def iota(shape, dim):
    return lax.broadcasted_iota(jnp.int32, shape, dim)


def dot(a, b):
    return jnp.dot(a, b, preferred_element_type=F32)


def onehot(match):
    return jnp.where(match, 1.0, 0.0).astype(BF16)


def across(column):
    return jnp.broadcast_to(column, (column.shape[0], 128))


def kernel(
    comps_in, entry_in, dest_in, slots_in, f0_in, x0_in, sens_in, cour_x_in, cour_y_in, diffusion_in, out,
    comps, entry, dest, slots, f0, x0, sens, cour_x, cour_y, diffusion, in_sem,
    send, recv, res, ret, tab_a, tab_xf, col_p, acc, halo_src, halo_dst, edge_src, edge_dst,
    fwd_send, fwd_recv, ret_send, ret_recv, tab_send, tab_recv, halo_send, halo_recv,
):
    me = lax.axis_index("wide")
    mine_n = lax.axis_index("narrow")
    z, y, c = me // 16, (me // 2) % SIDE, me % 2

    def at(dz, dy):
        return {"wide": ((z + dz) % SIDE) * 16 + ((y + dy) % SIDE) * 2 + c}

    def ahead(a, b):
        return at(far_first((a + SIDE - b) % SIDE), far_first(b))

    def behind(a, b):
        return at(SIDE - far_first((a + SIDE - b) % SIDE), SIDE - far_first(b))

    def each_group(step, last=SIDE):
        def body(a, carry):
            step(a, SIDE)
            return carry

        lax.fori_loop(0, SELF_GROUP, body, 0)
        step(SELF_GROUP, SIDE - 1)
        for a in range(SELF_GROUP + 1, last):
            step(a, SIDE)

    def remote(src, dst, send_sem, recv_sem, device):
        copy = pltpu.make_async_remote_copy(
            src_ref=src,
            dst_ref=dst,
            send_sem=send_sem,
            recv_sem=recv_sem,
            device_id=device,
            device_id_type=MESH,
        )
        copy.start()
        return copy

    def wait_for(ref, sem):
        pltpu.make_async_copy(ref, ref, sem).wait()

    partner = {"wide": me + 1 - 2 * c}
    above, below = {"wide": (me + 1) % 128}, {"wide": (me + 127) % 128}
    north, south = {"narrow": (mine_n + 1) % 4}, {"narrow": (mine_n + 3) % 4}

    loads = [
        pltpu.make_async_copy(src, dst, in_sem.at[n])
        for n, (src, dst) in enumerate(
            (
                (dest_in, dest),
                (entry_in, entry),
                (comps_in, comps),
                (slots_in, slots),
                (f0_in, f0),
                (x0_in, x0),
                (sens_in, sens),
                (cour_x_in, cour_x),
                (cour_y_in, cour_y),
                (diffusion_in, diffusion),
            )
        )
    ]
    for load in loads:
        load.start()

    recv[...] = jnp.zeros_like(recv)
    ret[...] = jnp.zeros_like(ret)
    tab_xf[pl.ds(32, 96), :] = jnp.zeros((96, 256), BF16)

    barrier = pltpu.get_barrier_semaphore()

    def greet(device):
        pl.semaphore_signal(barrier, inc=1, device_id=device, device_id_type=MESH)

    def greet_some(u, carry):
        for b in range(SIDE):
            greet(at(far_first(2 * (u % 4) + b // 4), far_first(4 * (u // 4) + b % 4)))
        return carry

    lax.fori_loop(0, SIDE - 1, greet_some, 0)
    for b in range(SIDE - 1):
        greet(at(far_first(6 + b // 4), far_first(4 + b % 4)))
    for device in (above, below, north, south, partner):
        greet(device)

    for load in loads:
        load.wait()

    owner = dest[...]
    matches = [iota((128, 128), 0) == owner[i : i + 1, :] for i in range(8)]
    owned = jnp.concatenate([onehot(m) for m in matches], axis=0)
    before = onehot(iota((128, 128), 0) < iota((128, 128), 1))
    counts = dot(owned, jnp.concatenate([before, jnp.ones((128, 128), BF16)], axis=1))
    carry = jnp.zeros((128, 128), F32)
    ranks = []
    for i in range(8):
        part = counts[i * 128 : (i + 1) * 128]
        seen = jnp.where(matches[i], part[:, :128] + carry, 0.0)
        ranks.append(jnp.sum(seen, axis=0, keepdims=True))
        carry = carry + part[:, 128:]
    rank = jnp.concatenate(ranks, axis=0).astype(jnp.int32)

    to_core = owner % 2
    i_y = rank_of_distance((owner // 2 + SIDE - y) % SIDE)
    i_z = rank_of_distance((owner // 16 + SIDE - z) % SIDE)
    slab = ((i_z + i_y) % SIDE) * SIDE + i_y
    row = to_core * CAP + rank
    place = slab * SLAB + row
    named = entry[...] + to_core * ENTRIES + 1

    place_t = jnp.transpose(place.astype(F32))
    row_t = jnp.transpose(row.astype(F32))
    named_t = jnp.transpose(named.astype(F32))
    lane = iota((128, 128), 1)
    lane_f = lane.astype(F32)
    names = []
    for i in range(8):
        col_p[pl.ds(i * 128, 128), :] = across(place_t[:, i : i + 1])
        names.append(jnp.where(across(row_t[:, i : i + 1]) == lane_f, across(named_t[:, i : i + 1]), 0.0))
    names = jnp.concatenate(names, axis=0).astype(BF16)
    in_slab = jnp.concatenate([onehot(iota((128, 128), 0) == slab[i : i + 1, :]) for i in range(8)], axis=1)
    entry_rows = dot(in_slab, names).astype(BF16)
    entry_place = jnp.where(lane[:1] < SLABS, lane[:1] * SLAB + ENTRY_ROW, -1)
    cells = jnp.concatenate([comps[...].reshape(1024, 128), entry_rows], axis=0)
    places = [place[i : i + 1, :] for i in range(8)] + [entry_place]

    pick = jnp.zeros((ENTRIES, 128), F32)
    for e in range(ENTRIES):
        s = slots[e]
        tab_a[c, pl.ds(e * 128, 128), :] = sens[s]
        pick = jnp.where((iota(pick.shape, 0) == e) & (iota(pick.shape, 1) == s), 1.0, pick)
    xf = jnp.concatenate([x0[...], f0[...]], axis=1)
    xf = jnp.concatenate([xf, jnp.zeros((112, 256), BF16)], axis=0)
    own_rows = pl.ds(pl.multiple_of(c * ENTRIES, ENTRIES), ENTRIES)
    tab_xf[own_rows, :] = dot(pick.astype(BF16), xf).astype(BF16)

    pl.semaphore_wait(barrier, SLABS - 1 + 5)

    swaps = [
        remote(ref, ref, tab_send.at[n], tab_recv.at[n], partner)
        for n, ref in enumerate((tab_a.at[c], tab_xf.at[own_rows]))
    ]

    def send_group(a, peers):
        slot = iota((GROUP, 128), 0) + a * GROUP
        chosen = jnp.concatenate([onehot(slot == p) for p in places], axis=1)
        send[pl.ds(a * 8, 8)] = dot(chosen, cells).astype(BF16).reshape(8, SLAB, 128)
        for b in range(peers):
            k = a * 8 + b
            sent = pl.ds(0, SENT)
            remote(send.at[k, sent], recv.at[k, sent], fwd_send, fwd_recv.at[a], ahead(a, b))

    each_group(send_group)
    recv[SELF] = send[SELF]
    for swap in swaps:
        swap.wait()

    wide_lane = iota((GROUP, 128), 1)
    in_own_row = wide_lane == iota((GROUP, 128), 0) % SLAB
    spread = onehot(iota((GROUP, GROUP), 1) == (iota((GROUP, GROUP), 0) // SLAB) * SLAB + ENTRY_ROW)
    all_ones = jnp.ones((128, 128), BF16)

    def map_group(a, peers):
        wait_for(recv.at[pl.ds(a * 8, peers), pl.ds(0, SENT)], fwd_recv.at[a])
        states = recv[pl.ds(a * 8, 8)].reshape(GROUP, 128)
        named = jnp.where(in_own_row, dot(spread, states), 0.0).astype(BF16)
        named = dot(named, all_ones)
        base = dot(onehot(named == (wide_lane + 1).astype(F32)), tab_xf[...])
        offset = (states.astype(F32) - base[:, :128]).astype(BF16)
        chosen = [
            jnp.where(named == float(e + 1), offset.astype(F32), 0.0).astype(BF16) for e in range(2 * ENTRIES)
        ]
        moved = dot(jnp.concatenate(chosen, axis=1), tab_a[...].reshape(2 * ENTRIES * 128, 128))
        res[pl.ds(a * 8, 8)] = (base[:, 128:] + moved).astype(BF16).reshape(8, SLAB, 128)
        for b in range(peers):
            k = a * 8 + b
            back = pl.ds(0, BACK)
            remote(res.at[k, back], ret.at[k, back], ret_send, ret_recv.at[a], behind(a, b))

    each_group(map_group)
    ret[SELF] = res[SELF]

    def placed(a, first, count):
        slot = (iota((count, 128), 1) + a * GROUP).astype(F32)
        at_col = col_p[pl.ds(first, count), :]
        chosen = jnp.concatenate([onehot(at_col == slot), onehot(at_col == slot + 128.0)], axis=1)
        return dot(chosen, ret[pl.ds(a * 8, 8)].reshape(GROUP, 128))

    acc[...] = jnp.zeros_like(acc)

    def place_group(a, peers):
        wait_for(ret.at[pl.ds(a * 8, peers), pl.ds(0, BACK)], ret_recv.at[a])
        acc[...] += placed(a, 0, 1024)

    last = SIDE - 1
    each_group(place_group, last)
    wait_for(ret.at[pl.ds(last * 8, 8), pl.ds(0, BACK)], ret_recv.at[last])

    def finish(first, count):
        done = acc[pl.ds(first, count), :] + placed(last, first, count)
        acc[pl.ds(first, count), :] = done
        return done

    def halo(n, src, dst, device):
        return remote(src, dst, halo_send.at[n], halo_recv.at[n], device)

    halo_src[0] = finish(0, 128).astype(BF16)
    halos = [halo(0, halo_src.at[0], halo_dst.at[1], below)]
    halo_src[1] = finish(896, 128).astype(BF16)
    halos.append(halo(1, halo_src.at[1], halo_dst.at[0], above))
    finish(128, 768)
    field = [acc[pl.ds(i * 128, 128), :] for i in range(8)]
    edge_src[0] = jnp.concatenate([p[:1] for p in field], axis=0)
    edge_src[1] = jnp.concatenate([p[127:] for p in field], axis=0)
    halos.append(halo(2, edge_src.at[0], edge_dst.at[1], south))
    halos.append(halo(3, edge_src.at[1], edge_dst.at[0], north))

    species = diffusion[...]
    cx_t = jnp.transpose(cour_x[...])
    cy_t = jnp.transpose(cour_y[...])
    nothing = jnp.zeros((128, 128), F32)
    no_row = jnp.zeros((1, 128), F32)
    for i in range(8):
        p = field[i]
        west = field[i - 1] if i > 0 else nothing
        east = field[i + 1] if i < 7 else nothing
        pn = jnp.concatenate([p[1:], no_row], axis=0)
        ps = jnp.concatenate([no_row, p[:127]], axis=0)
        cx, cy = across(cx_t[:, i : i + 1]), across(cy_t[:, i : i + 1])
        r = p - 0.5 * cx * (east - west) + (0.5 * cx * cx + species) * (east - 2.0 * p + west)
        out[i] = r - 0.5 * cy * (pn - ps) + (0.5 * cy * cy + species) * (pn - 2.0 * p + ps)

    for copy in halos:
        copy.wait()

    def weight(courant, sign):
        return sign * 0.5 * courant + 0.5 * courant * courant + species

    low = jnp.where(me > 0, halo_dst[0].astype(F32), 0.0)
    high = jnp.where(me < 127, halo_dst[1].astype(F32), 0.0)
    edge_s = jnp.where(mine_n > 0, edge_dst[0], 0.0)
    edge_n = jnp.where(mine_n < 3, edge_dst[1], 0.0)
    out[0] += low * weight(across(cx_t[:, 0:1]), 1.0)
    out[7] += high * weight(across(cx_t[:, 7:8]), -1.0)
    edge_s = edge_s * weight(across(cour_y[:, 0:1]), 1.0)
    edge_n = edge_n * weight(across(cour_y[:, 127:128]), -1.0)
    for i in range(8):
        out[i, 0:1, :] += edge_s[i : i + 1]
        out[i, 127:128, :] += edge_n[i : i + 1]

    for first, count in ((0, SELF), (SELF + 1, SLABS - SELF - 1)):
        wait_for(send.at[pl.ds(first, count), pl.ds(0, SENT)], fwd_send)
        wait_for(res.at[pl.ds(first, count), pl.ds(0, BACK)], ret_send)


def body(comps, entry, dest, slot_of_entry, table_f0, table_x0, table_a, courant_x, courant_y, diffusion):
    args = (
        comps,
        entry,
        dest.reshape(entry.shape),
        slot_of_entry.reshape(ENTRIES),
        table_f0[0, 0],
        table_x0[0, 0],
        table_a[0, 0],
        courant_x,
        courant_y,
        diffusion.reshape(1, -1),
    )
    hbm = pl.BlockSpec(memory_space=pltpu.HBM)
    dma = pltpu.SemaphoreType.DMA
    return pl.pallas_call(
        kernel,
        out_shape=jax.ShapeDtypeStruct(comps.shape, F32),
        in_specs=[hbm] * len(args),
        out_specs=pl.BlockSpec(memory_space=pltpu.VMEM),
        scratch_shapes=[
            pltpu.SMEM(a.shape, a.dtype) if n == 3 else pltpu.VMEM(a.shape, a.dtype) for n, a in enumerate(args)
        ]
        + [
            dma((len(args),)),
            pltpu.VMEM((SLABS, SLAB, 128), BF16),
            pltpu.VMEM((SLABS, SLAB, 128), BF16),
            pltpu.VMEM((SLABS, SLAB, 128), BF16),
            pltpu.VMEM((SLABS, SLAB, 128), BF16),
            pltpu.VMEM((2, ENTRIES * 128, 128), BF16),
            pltpu.VMEM((128, 256), BF16),
            pltpu.VMEM((1024, 128), F32),
            pltpu.VMEM((1024, 128), F32),
            pltpu.VMEM((2, 128, 128), BF16),
            pltpu.VMEM((2, 128, 128), BF16),
            pltpu.VMEM((2, 8, 128), F32),
            pltpu.VMEM((2, 8, 128), F32),
            dma(()),
            dma((SIDE,)),
            dma(()),
            dma((SIDE,)),
            dma((2,)),
            dma((2,)),
            dma((4,)),
            dma((4,)),
        ],
        compiler_params=pltpu.CompilerParams(
            collective_id=0, has_side_effects=True, vmem_limit_bytes=32 * 1024 * 1024
        ),
        name="chemistry",
    )(*[pltpu.with_memory_space_constraint(a, pltpu.HBM) for a in args])


def solution(mesh):
    in_specs = (
        P("wide", "narrow", None),
        P("wide", "narrow"),
        P("wide", "narrow", None, None),
        P("wide", "narrow", None),
        P("wide", "narrow", None, None),
        P("wide", "narrow", None, None),
        P("wide", "narrow", None, None, None),
        P("wide", "narrow"),
        P("wide", "narrow"),
        P(),
    )
    out_specs = P("wide", "narrow", None)
    return jax.shard_map(body, mesh=mesh, in_specs=in_specs, out_specs=out_specs, check_vma=False)
```

time: 52.8 us -> 44.9 us (0.85)
  local copies, waits for them, and re-layouts: 6.23 us -> 0.8 us
  Pallas kernels: 46.1 us -> 43.6 us
    unnamed x21 -> x1, local copies, waits for them, and re-layouts: 6.23 us -> 0.8 us
    pallas_call x1, Pallas kernels: 46.1 us -> 43.6 us  [body(): pl.pallas_call(kernel, out_shape=jax.ShapeDtypeStruct(comps.shape, F32),...]
where the time goes in v2:
time: 44.9 us; the launch traced here: 44.4 us
  Pallas kernels  43.6 us (97%)
  local copies, waits for them, and re-layouts  0.8 us (2%)
    pallas_call x1, Pallas kernels, body(): pl.pallas_call(kernel, out_shape=jax.ShapeDtypeStruct(comps.shape, F32),...  43.6 us

profile of v2, /device:TPU:1, one launch (start us, length us, event | category | flops | bytes accessed | tf_op | source)
XLA Modules:
  0.0 44.4 jit_solution(10534443726310546257)
XLA Ops:
  0.0 43.6 %chemistry.1 = f32[8,128,128]{2,1,0:T(8,128)S(1)} custom-call(bf16[8,128,128]{2,1,0:T(8,128)(2,1)} %comps_in.1, s32[8,128]{1,0:T(8,128)} %entry_in.1, s32[8,128]{1,0:T(8,128)} %bitcast.7, s32[16]{0:T(128)} %bitcast.10, bf16[16,128]{1,0:T(8,128)(2,1)} %bitcast.8, bf16[16,128]{1,0:T(8,128)(2,1)} %bitcast.9, bf16[16,128,128]{2,1,0:T(8,128)(2,1)} %bitcast.6, ...), custom_call_target="tpu_custom_call" | custom-call | tf_op jit(solution)/shard_map/chemistry/pallas_call | solution.py:324
  43.6 0.8 %copy.12 = f32[8,128,128]{2,1,0:T(8,128)} copy(f32[8,128,128]{2,1,0:T(8,128)S(1)} %chemistry.1) | data formatting | bytes 1048576

commit v3 on v2

--- a/solution.py
+++ b/solution.py
@@ -10,8 +10,24 @@
 BF16 = jnp.bfloat16
 
 SIDE = 8
-SELF = 55
-SELF_GROUP = SELF // SIDE
+
+
+def hops(offset):
+    return [min(d, SIDE - d) for d in offset]
+
+
+def longest_first(offset):
+    far, (dz, dy) = hops(offset), offset
+    return (-sum(far), -max(far), far[0] > far[1], (dz > SIDE // 2) != (dy > SIDE // 2), dz, dy)
+
+
+OTHERS = sorted([(dz, dy) for dz in range(SIDE) for dy in range(SIDE) if (dz, dy) != (0, 0)], key=longest_first)
+NEAR = [o for o in OTHERS if sum(hops(o)) <= 3]
+OFFSETS = NEAR + [o for o in OTHERS if o not in NEAR] + [(0, 0)]
+NEAR_GROUPS = len(NEAR) // SIDE
+COLUMN = [o for o in OTHERS if o[1] == 0]
+FIRST = [o for o in OTHERS if o in NEAR or 0 in o]
+SELF = len(OFFSETS) - 1
 CAP = 12
 SLAB = 32
 SENT = 26
@@ -22,16 +38,6 @@
 ENTRIES = 16
 
 
-def far_first(i):
-    odd = i % 2
-    return (4 + odd * ((i + 1) // 2) + (1 - odd) * (8 - i // 2)) % SIDE
-
-
-def rank_of_distance(d):
-    t = lax.rem(d + 7, SIDE) - 3
-    return jnp.where(t > 0, 2 * t - 1, -2 * t)
-
-
 def iota(shape, dim):
     return lax.broadcasted_iota(jnp.int32, shape, dim)
 
@@ -52,30 +58,33 @@
     comps_in, entry_in, dest_in, slots_in, f0_in, x0_in, sens_in, cour_x_in, cour_y_in, diffusion_in, out,
     comps, entry, dest, slots, f0, x0, sens, cour_x, cour_y, diffusion, in_sem,
     send, recv, res, ret, tab_a, tab_xf, col_p, acc, halo_src, halo_dst, edge_src, edge_dst,
-    fwd_send, fwd_recv, ret_send, ret_recv, tab_send, tab_recv, halo_send, halo_recv,
+    fwd_send, fwd_recv, ret_send, ret_recv, tab_send, tab_recv, halo_send, halo_recv, row_in,
 ):
     me = lax.axis_index("wide")
     mine_n = lax.axis_index("narrow")
     z, y, c = me // 16, (me // 2) % SIDE, me % 2
 
+    rows_z = [(z + d) % SIDE * 16 for d in range(SIDE)]
+    rows_y = [(y + d) % SIDE * 2 + c for d in range(SIDE)]
+
     def at(dz, dy):
-        return {"wide": ((z + dz) % SIDE) * 16 + ((y + dy) % SIDE) * 2 + c}
-
-    def ahead(a, b):
-        return at(far_first((a + SIDE - b) % SIDE), far_first(b))
+        return {"wide": rows_z[dz % SIDE] + rows_y[dy % SIDE]}
 
     def behind(a, b):
-        return at(SIDE - far_first((a + SIDE - b) % SIDE), SIDE - far_first(b))
+        dz, dy = OFFSETS[b]
+        for g in range(1, SIDE):
+            dz = jnp.where(a == g, OFFSETS[g * 8 + b][0], dz)
+            dy = jnp.where(a == g, OFFSETS[g * 8 + b][1], dy)
+        return {"wide": (z + SIDE - dz) % SIDE * 16 + (y + SIDE - dy) % SIDE * 2 + c}
 
     def each_group(step, last=SIDE):
         def body(a, carry):
             step(a, SIDE)
             return carry
 
-        lax.fori_loop(0, SELF_GROUP, body, 0)
-        step(SELF_GROUP, SIDE - 1)
-        for a in range(SELF_GROUP + 1, last):
-            step(a, SIDE)
+        lax.fori_loop(0, SIDE - 1, body, 0)
+        if last == SIDE:
+            step(SIDE - 1, SIDE - 1)
 
     def remote(src, dst, send_sem, recv_sem, device):
         copy = pltpu.make_async_remote_copy(
@@ -117,26 +126,20 @@
         load.start()
 
     recv[...] = jnp.zeros_like(recv)
+
+    barrier = pltpu.get_barrier_semaphore()
+
+    def greet(device):
+        pl.semaphore_signal(barrier, inc=1, device_id=device, device_id_type=MESH)
+
+    for offset in FIRST:
+        greet(at(*offset))
+    for device in (above, below, north, south, partner):
+        greet(device)
+
     ret[...] = jnp.zeros_like(ret)
     tab_xf[pl.ds(32, 96), :] = jnp.zeros((96, 256), BF16)
-
-    barrier = pltpu.get_barrier_semaphore()
-
-    def greet(device):
-        pl.semaphore_signal(barrier, inc=1, device_id=device, device_id_type=MESH)
-
-    def greet_some(u, carry):
-        for b in range(SIDE):
-            greet(at(far_first(2 * (u % 4) + b // 4), far_first(4 * (u // 4) + b % 4)))
-        return carry
-
-    lax.fori_loop(0, SIDE - 1, greet_some, 0)
-    for b in range(SIDE - 1):
-        greet(at(far_first(6 + b // 4), far_first(4 + b % 4)))
-    for device in (above, below, north, south, partner):
-        greet(device)
-
-    for load in loads:
+    for load in loads[:3]:
         load.wait()
 
     owner = dest[...]
@@ -154,9 +157,10 @@
     rank = jnp.concatenate(ranks, axis=0).astype(jnp.int32)
 
     to_core = owner % 2
-    i_y = rank_of_distance((owner // 2 + SIDE - y) % SIDE)
-    i_z = rank_of_distance((owner // 16 + SIDE - z) % SIDE)
-    slab = ((i_z + i_y) % SIDE) * SIDE + i_y
+    offset = (owner // 16 + SIDE - z) % SIDE * SIDE + (owner // 2 + SIDE - y) % SIDE
+    slab = jnp.zeros_like(owner)
+    for k, (dz, dy) in enumerate(OFFSETS):
+        slab = jnp.where(offset == dz * SIDE + dy, k, slab)
     row = to_core * CAP + rank
     place = slab * SLAB + row
     named = entry[...] + to_core * ENTRIES + 1
@@ -177,6 +181,29 @@
     cells = jnp.concatenate([comps[...].reshape(1024, 128), entry_rows], axis=0)
     places = [place[i : i + 1, :] for i in range(8)] + [entry_place]
 
+    def pack(a, carry):
+        slot = iota((GROUP, 128), 0) + a * GROUP
+        chosen = jnp.concatenate([onehot(slot == p) for p in places], axis=1)
+        send[pl.ds(a * 8, 8)] = dot(chosen, cells).astype(BF16).reshape(8, SLAB, 128)
+        return carry
+
+    lax.fori_loop(0, NEAR_GROUPS, pack, 0)
+
+    pl.semaphore_wait(barrier, len(FIRST) + 5)
+
+    for offset in COLUMN:
+        pl.semaphore_signal(row_in, inc=1, device_id=at(*offset), device_id_type=MESH)
+
+    def send_groups(first, last):
+        sent = pl.ds(0, SENT)
+        for k in range(first * 8, min(last * 8, SELF)):
+            remote(send.at[k, sent], recv.at[k, sent], fwd_send, fwd_recv.at[k // 8], at(*OFFSETS[k]))
+
+    send_groups(0, NEAR_GROUPS)
+
+    for load in loads[3:]:
+        load.wait()
+
     pick = jnp.zeros((ENTRIES, 128), F32)
     for e in range(ENTRIES):
         s = slots[e]
@@ -187,24 +214,15 @@
     own_rows = pl.ds(pl.multiple_of(c * ENTRIES, ENTRIES), ENTRIES)
     tab_xf[own_rows, :] = dot(pick.astype(BF16), xf).astype(BF16)
 
-    pl.semaphore_wait(barrier, SLABS - 1 + 5)
-
     swaps = [
         remote(ref, ref, tab_send.at[n], tab_recv.at[n], partner)
         for n, ref in enumerate((tab_a.at[c], tab_xf.at[own_rows]))
     ]
 
-    def send_group(a, peers):
-        slot = iota((GROUP, 128), 0) + a * GROUP
-        chosen = jnp.concatenate([onehot(slot == p) for p in places], axis=1)
-        send[pl.ds(a * 8, 8)] = dot(chosen, cells).astype(BF16).reshape(8, SLAB, 128)
-        for b in range(peers):
-            k = a * 8 + b
-            sent = pl.ds(0, SENT)
-            remote(send.at[k, sent], recv.at[k, sent], fwd_send, fwd_recv.at[a], ahead(a, b))
-
-    each_group(send_group)
+    lax.fori_loop(NEAR_GROUPS, SIDE, pack, 0)
     recv[SELF] = send[SELF]
+    pl.semaphore_wait(row_in, len(COLUMN))
+    send_groups(NEAR_GROUPS, SIDE)
     for swap in swaps:
         swap.wait()
 
@@ -220,9 +238,8 @@
         named = dot(named, all_ones)
         base = dot(onehot(named == (wide_lane + 1).astype(F32)), tab_xf[...])
         offset = (states.astype(F32) - base[:, :128]).astype(BF16)
-        chosen = [
-            jnp.where(named == float(e + 1), offset.astype(F32), 0.0).astype(BF16) for e in range(2 * ENTRIES)
-        ]
+        names = named.astype(BF16)
+        chosen = [jnp.where(names == jnp.bfloat16(e + 1), offset, jnp.bfloat16(0)) for e in range(2 * ENTRIES)]
         moved = dot(jnp.concatenate(chosen, axis=1), tab_a[...].reshape(2 * ENTRIES * 128, 128))
         res[pl.ds(a * 8, 8)] = (base[:, 128:] + moved).astype(BF16).reshape(8, SLAB, 128)
         for b in range(peers):
@@ -247,7 +264,7 @@
 
     last = SIDE - 1
     each_group(place_group, last)
-    wait_for(ret.at[pl.ds(last * 8, 8), pl.ds(0, BACK)], ret_recv.at[last])
+    wait_for(ret.at[pl.ds(last * 8, 7), pl.ds(0, BACK)], ret_recv.at[last])
 
     def finish(first, count):
         done = acc[pl.ds(first, count), :] + placed(last, first, count)
@@ -301,9 +318,8 @@
         out[i, 0:1, :] += edge_s[i : i + 1]
         out[i, 127:128, :] += edge_n[i : i + 1]
 
-    for first, count in ((0, SELF), (SELF + 1, SLABS - SELF - 1)):
-        wait_for(send.at[pl.ds(first, count), pl.ds(0, SENT)], fwd_send)
-        wait_for(res.at[pl.ds(first, count), pl.ds(0, BACK)], ret_send)
+    wait_for(send.at[pl.ds(0, SELF), pl.ds(0, SENT)], fwd_send)
+    wait_for(res.at[pl.ds(0, SELF), pl.ds(0, BACK)], ret_send)
 
 
 def body(comps, entry, dest, slot_of_entry, table_f0, table_x0, table_a, courant_x, courant_y, diffusion):
@@ -351,6 +367,7 @@
             dma((2,)),
             dma((4,)),
             dma((4,)),
+            pltpu.SemaphoreType.REGULAR,
         ],
         compiler_params=pltpu.CompilerParams(
             collective_id=0, has_side_effects=True, vmem_limit_bytes=32 * 1024 * 1024

time: 44.9 us -> 42.5 us (0.947)
  Pallas kernels: 43.6 us -> 41.1 us
    pallas_call x1, Pallas kernels: 43.6 us -> 41.1 us  [body(): pl.pallas_call(kernel, out_shape=jax.ShapeDtypeStruct(comps.shape, F32),...]
where the time goes in v3:
time: 42.5 us; the launch traced here: 41.9 us
  Pallas kernels  41.1 us (97%)
  local copies, waits for them, and re-layouts  0.8 us (2%)
    pallas_call x1, Pallas kernels, body(): pl.pallas_call(kernel, out_shape=jax.ShapeDtypeStruct(comps.shape, F32),...  41.1 us

profile of v3, /device:TPU:1, one launch (start us, length us, event | category | flops | bytes accessed | tf_op | source)
XLA Modules:
  0.0 41.9 jit_solution(6221650981602675330)
XLA Ops:
  0.0 41.1 %chemistry.1 = f32[8,128,128]{2,1,0:T(8,128)S(1)} custom-call(bf16[8,128,128]{2,1,0:T(8,128)(2,1)} %comps_in.1, s32[8,128]{1,0:T(8,128)} %entry_in.1, s32[8,128]{1,0:T(8,128)} %bitcast.7, s32[16]{0:T(128)} %bitcast.10, bf16[16,128]{1,0:T(8,128)(2,1)} %bitcast.8, bf16[16,128]{1,0:T(8,128)(2,1)} %bitcast.9, bf16[16,128,128]{2,1,0:T(8,128)(2,1)} %bitcast.6, ...), custom_call_target="tpu_custom_call" | custom-call | tf_op jit(solution)/shard_map/chemistry/pallas_call | solution.py:340
  41.1 0.8 %copy.12 = f32[8,128,128]{2,1,0:T(8,128)} copy(f32[8,128,128]{2,1,0:T(8,128)S(1)} %chemistry.1) | data formatting | bytes 1048576

commit v4 on v3

--- a/solution.py
+++ b/solution.py
@@ -165,18 +165,16 @@
     place = slab * SLAB + row
     named = entry[...] + to_core * ENTRIES + 1
 
-    place_t = jnp.transpose(place.astype(F32))
-    row_t = jnp.transpose(row.astype(F32))
-    named_t = jnp.transpose(named.astype(F32))
     lane = iota((128, 128), 1)
-    lane_f = lane.astype(F32)
-    names = []
-    for i in range(8):
-        col_p[pl.ds(i * 128, 128), :] = across(place_t[:, i : i + 1])
-        names.append(jnp.where(across(row_t[:, i : i + 1]) == lane_f, across(named_t[:, i : i + 1]), 0.0))
-    names = jnp.concatenate(names, axis=0).astype(BF16)
-    in_slab = jnp.concatenate([onehot(iota((128, 128), 0) == slab[i : i + 1, :]) for i in range(8)], axis=1)
-    entry_rows = dot(in_slab, names).astype(BF16)
+    in_slab = [iota((128, 128), 0) == slab[i : i + 1, :] for i in range(8)]
+    in_slab = [jnp.where(m, named[i : i + 1, :].astype(F32), 0.0).astype(BF16) for i, m in enumerate(in_slab)]
+    in_row = [onehot(iota((128, 128), 0) == row[i : i + 1, :]) for i in range(8)]
+    entry_rows = lax.dot_general(
+        jnp.concatenate(in_slab, axis=1),
+        jnp.concatenate(in_row, axis=1),
+        (((1,), (1,)), ((), ())),
+        preferred_element_type=F32,
+    ).astype(BF16)
     entry_place = jnp.where(lane[:1] < SLABS, lane[:1] * SLAB + ENTRY_ROW, -1)
     cells = jnp.concatenate([comps[...].reshape(1024, 128), entry_rows], axis=0)
     places = [place[i : i + 1, :] for i in range(8)] + [entry_place]
@@ -221,6 +219,9 @@
 
     lax.fori_loop(NEAR_GROUPS, SIDE, pack, 0)
     recv[SELF] = send[SELF]
+    place_t = jnp.transpose(place.astype(F32))
+    for i in range(8):
+        col_p[pl.ds(i * 128, 128), :] = across(place_t[:, i : i + 1])
     pl.semaphore_wait(row_in, len(COLUMN))
     send_groups(NEAR_GROUPS, SIDE)
     for swap in swaps:
@@ -250,35 +251,38 @@
     each_group(map_group)
     ret[SELF] = res[SELF]
 
-    def placed(a, first, count):
+    def chosen_for(a, first, count):
         slot = (iota((count, 128), 1) + a * GROUP).astype(F32)
         at_col = col_p[pl.ds(first, count), :]
-        chosen = jnp.concatenate([onehot(at_col == slot), onehot(at_col == slot + 128.0)], axis=1)
+        return jnp.concatenate([onehot(at_col == slot), onehot(at_col == slot + 128.0)], axis=1)
+
+    def placed(a, chosen):
         return dot(chosen, ret[pl.ds(a * 8, 8)].reshape(GROUP, 128))
 
     acc[...] = jnp.zeros_like(acc)
 
     def place_group(a, peers):
         wait_for(ret.at[pl.ds(a * 8, peers), pl.ds(0, BACK)], ret_recv.at[a])
-        acc[...] += placed(a, 0, 1024)
+        acc[...] += placed(a, chosen_for(a, 0, 1024))
 
     last = SIDE - 1
     each_group(place_group, last)
+    outer = [chosen_for(last, first, 128) for first in (0, 896)]
     wait_for(ret.at[pl.ds(last * 8, 7), pl.ds(0, BACK)], ret_recv.at[last])
 
-    def finish(first, count):
-        done = acc[pl.ds(first, count), :] + placed(last, first, count)
+    def finish(first, count, chosen):
+        done = acc[pl.ds(first, count), :] + placed(last, chosen)
         acc[pl.ds(first, count), :] = done
         return done
 
     def halo(n, src, dst, device):
         return remote(src, dst, halo_send.at[n], halo_recv.at[n], device)
 
-    halo_src[0] = finish(0, 128).astype(BF16)
+    halo_src[0] = finish(0, 128, outer[0]).astype(BF16)
     halos = [halo(0, halo_src.at[0], halo_dst.at[1], below)]
-    halo_src[1] = finish(896, 128).astype(BF16)
+    halo_src[1] = finish(896, 128, outer[1]).astype(BF16)
     halos.append(halo(1, halo_src.at[1], halo_dst.at[0], above))
-    finish(128, 768)
+    finish(128, 768, chosen_for(last, 128, 768))
     field = [acc[pl.ds(i * 128, 128), :] for i in range(8)]
     edge_src[0] = jnp.concatenate([p[:1] for p in field], axis=0)
     edge_src[1] = jnp.concatenate([p[127:] for p in field], axis=0)

time: 42.5 us -> 42.5 us (level)
  no operation moved by 1% of the time
where the time goes in v4:
time: 42.5 us; the launch traced here: 41.9 us
  Pallas kernels  41.1 us (97%)
  local copies, waits for them, and re-layouts  0.8 us (2%)
    pallas_call x1, Pallas kernels, body(): pl.pallas_call(kernel, out_shape=jax.ShapeDtypeStruct(comps.shape, F32),...  41.1 us

profile of v4, /device:TPU:1, one launch (start us, length us, event | category | flops | bytes accessed | tf_op | source)
XLA Modules:
  0.0 41.9 jit_solution(7630165942050114294)
XLA Ops:
  0.0 41.1 %chemistry.1 = f32[8,128,128]{2,1,0:T(8,128)S(1)} custom-call(bf16[8,128,128]{2,1,0:T(8,128)(2,1)} %comps_in.1, s32[8,128]{1,0:T(8,128)} %entry_in.1, s32[8,128]{1,0:T(8,128)} %bitcast.7, s32[16]{0:T(128)} %bitcast.10, bf16[16,128]{1,0:T(8,128)(2,1)} %bitcast.8, bf16[16,128]{1,0:T(8,128)(2,1)} %bitcast.9, bf16[16,128,128]{2,1,0:T(8,128)(2,1)} %bitcast.6, ...), custom_call_target="tpu_custom_call" | custom-call | tf_op jit(solution)/shard_map/chemistry/pallas_call | solution.py:344
  41.1 0.8 %copy.12 = f32[8,128,128]{2,1,0:T(8,128)} copy(f32[8,128,128]{2,1,0:T(8,128)S(1)} %chemistry.1) | data formatting | bytes 1048576
